TPU v7x, 32 devices: a whole 2x2x4 slice. The times are simulated.
32 devices in a mesh: grp: 2 (over y), site: 4 (over x, core), spin: 4 (over z).
Axes of the slice: x: 2, y: 2, z: 4, core: 2. Of those that a mesh axis runs over, the one named last changes fastest.
Arguments:
- walkers: bfloat16 [8, 512, 256, 256], P(('grp', 'spin'), 'site'), parts along dimension 0, may hold values from -90 to 90
- fields: bfloat16 [8, 1, 512, 256], P(('grp', 'spin'), None, 'site'), parts along dimension 0, may hold values from -3 to 3
- kinetic_x: bfloat16 [512, 512], replicated, may hold values from -0.5 to 1.5
- kinetic_y: bfloat16 [256, 256], replicated, may hold values from -0.5 to 1.5
Outputs:
- orthonormal: bfloat16 [8, 512, 256, 256], P(('grp', 'spin'), 'site'), parts along dimension 0
- triangle: float32 [8, 256, 256], P(('grp', 'spin')), parts along dimension 0
There are 2 independent parts, one for each index of `grp`. A program takes and returns all parts, laid end to end along the dimension named above; an argument that names none is the same for every part. Nothing has to cross between parts.
All inputs are finite; a program needn't handle non-finite values.
Results may differ from a plain program's by a relative error of at most 0.0095.
Values may be sent and summed in bfloat16 or wider, within the bound.
No kernel may reach another device: no remote copies, remote signals or barrier semaphores. Data moves between devices by JAX's collectives and lax.ppermute only.
A program may use at most 128 MiB of HBM per device.

v0:
```python
import jax
import jax.numpy as jnp
from jax import lax
from jax.sharding import PartitionSpec as P

LX = 512
LY = 256


def apply_y(current, kinetic_y):
    return jnp.einsum(
        "yz,sxzm->sxym", kinetic_y, current, preferred_element_type=jnp.float32
    ).astype(jnp.bfloat16)


def apply_x(current, kinetic_x):
    return jnp.einsum(
        "xz,szym->sxym", kinetic_x, current, preferred_element_type=jnp.float32
    ).astype(jnp.bfloat16)


def scale_sites(current, field):
    factor = jnp.exp(field.astype(jnp.float32))
    return (factor[..., None] * current.astype(jnp.float32)).astype(jnp.bfloat16)


def per_device(walkers, fields, kinetic_x, kinetic_y):
    current = walkers
    every_field = lax.all_gather(fields, "site", axis=2, tiled=True)
    moved = lax.all_to_all(
        apply_y(current, kinetic_y), "site", split_axis=3, concat_axis=1, tiled=True
    )
    moved = scale_sites(apply_x(moved, kinetic_x), every_field[:, 0])
    current = lax.all_to_all(moved, "site", split_axis=1, concat_axis=3, tiled=True)
    slots = current.shape[0]
    orbitals = current.shape[3]
    flat = current.reshape(slots, -1, orbitals)
    local_gram = jnp.einsum("snm,snk->smk", flat, flat, preferred_element_type=jnp.float32) * (
        1.0 / (LX * LY)
    )
    lower = jnp.linalg.cholesky(lax.psum(local_gram, "site"))
    identity = jnp.broadcast_to(jnp.eye(orbitals, dtype=jnp.float32), lower.shape)
    inverse = jnp.swapaxes(jax.scipy.linalg.solve_triangular(lower, identity, lower=True), 1, 2)
    inverse_half = inverse.astype(jnp.bfloat16)
    result = jnp.einsum(
        "snm,smk->snk", flat, inverse_half, preferred_element_type=jnp.float32
    ).astype(jnp.bfloat16)
    return (result.reshape(current.shape), lower)


def solution(mesh):
    placed = (
        P(("grp", "spin"), "site", None, None),
        P(("grp", "spin"), None, "site", None),
        P(),
        P(),
    )
    return jax.shard_map(
        per_device,
        mesh=mesh,
        in_specs=placed,
        out_specs=(P(("grp", "spin"), "site", None, None), P(("grp", "spin"), None, None)),
        check_vma=False,
    )
```

profile of v0, /device:TPU:1, one launch (start us, length us, event | category | flops | bytes accessed | tf_op | source)
XLA Modules:
  0.0 672.7 jit_solution(17338018074648573066)
XLA Ops:
  7.2 0.0 copy-start
  7.2 12.0 %convert_bitcast_fusion.1 = bf16[1,128,256,256]{2,3,1,0:T(8,128)(2,1)} fusion(bf16[1,128,256,256]{3,2,1,0:T(8,128)(2,1)} %param.4, bf16[256,256]{1,0:T(8,128)(2,1)} %param.7), kind=kOutput, calls=%fused_computation.8 | convolution fusion | flops 4303355904 | bytes 33685504 | tf_op jit(solution)/shard_map/yz,sxzm->sxym/dot_general | solution.py:11
  19.2 17.9 %copy.19 = bf16[1,128,256,256]{2,1,0,3:T(8,128)(2,1)} copy(bf16[1,128,256,256]{2,3,1,0:T(8,128)(2,1)} %convert_bitcast_fusion.1) | data formatting | bytes 33554432 | tf_op jit(solution)/shard_map/convert_element_type | solution.py:13
  37.1 0.0 copy-start.2
  37.1 7.1 %all-to-all-start = ((bf16[1,128,256,256]{2,1,0,3:T(8,128)(2,1)}), bf16[1,128,256,256]{2,1,0,3:T(8,128)(2,1)}, u32[]{:S(2)}, u32[]{:S(2)}) async-start(bf16[1,128,256,256]{2,1,0,3:T(8,128)(2,1)} %copy.19), calls=%async_computation | async-start | bytes 33554432 | tf_op jit(solution)/shard_map/all_to_all | solution.py:30
  44.3 0.0 all-reduce.3.cloned.1.call-start
  44.3 0.0 copy-done.2
  44.3 185.6 %all_gather.3 = bf16[1,1,512,256]{3,2,1,0:T(8,128)(2,1)S(1)} all-gather(bf16[1,1,128,256]{3,2,1,0:T(8,128)(2,1)S(1)} %copy-done.2), channel_id=1, replica_groups=mesh['grp'=2,'site'=4,'spin'=4] {'site'}, dimensions={2}, use_global_device_ids=true | all-gather | bytes 327680 | tf_op jit(solution)/shard_map/all_gather | solution.py:29
  230.0 0.1 exponential_bitcast_fusion
  230.0 0.2 copy.17
  230.2 0.0 all-to-all-done
  230.2 25.8 %copy.20 = bf16[1,128,256,4,64]{1,3,2,4,0:T(4,128)(2,1)} copy(bf16[1,128,256,4,64]{2,1,4,3,0:T(8,128)(2,1)} %bitcast.5) | data formatting | bytes 33554432 | tf_op jit(solution)/shard_map/all_to_all | solution.py:30
  256.0 24.9 %reshape.138 = bf16[512,256,64]{0,1,2:T(8,128)(2,1)} reshape(bf16[1,4,128,256,64]{2,1,3,4,0:T(4,128)(2,1)} %bitcast.99) | data formatting | bytes 33554432 | tf_op jit(solution)/shard_map/reshape.20
  280.9 0.0 copy-done
  280.9 18.3 %fusion.1 = bf16[1,512,256,64]{1,2,3,0:T(8,128)(2,1)} fusion(f32[512,256]{0,1:T(8,128)S(1)} %copy.17, bf16[512,256,64]{0,1,2:T(8,128)(2,1)} %reshape.138, bf16[512,512]{1,0:T(8,128)(2,1)S(1)} %copy-done), kind=kOutput, calls=%fused_computation.5 | convolution fusion | flops 8623489024 | bytes 34603008 | tf_op jit(solution)/shard_map/xz,szym->sxym/dot_general | solution.py:17
  299.2 23.4 %copy.21 = bf16[1,512,256,64]{2,3,0,1:T(8,128)(2,1)} copy(bf16[1,512,256,64]{1,2,3,0:T(8,128)(2,1)} %fusion.1) | data formatting | bytes 33554432 | tf_op jit(solution)/shard_map/convert_element_type | solution.py:24
  322.6 186.8 %all_to_all.30 = bf16[1,512,256,64]{2,3,0,1:T(8,128)(2,1)S(1)} all-to-all(bf16[1,512,256,64]{2,3,0,1:T(8,128)(2,1)} %copy.21), channel_id=1, replica_groups=mesh['grp'=2,'site'=4,'spin'=4] {'site'}, dimensions={1} | all-to-all | bytes 33554432 | tf_op jit(solution)/shard_map/all_to_all | solution.py:34
  509.5 21.7 %copy.22 = bf16[1,4,128,256,64]{3,2,4,1,0:T(8,128)(2,1)S(1)} copy(bf16[1,4,128,256,64]{3,4,2,1,0:T(8,128)(2,1)S(1)} %bitcast.100) | data formatting | bytes 33554432 | tf_op jit(solution)/shard_map/all_to_all | solution.py:34
  531.2 11.4 %copy.27 = bf16[32,8,128,256]{3,1,2,0:T(8,128)(2,1)} copy(bf16[32,8,128,256]{3,2,1,0:T(8,128)(2,1)S(1)} %bitcast.101) | data formatting | bytes 33554432
  542.6 15.8 %fusion.6 = f32[1,256,256]{1,2,0:T(8,128)} fusion(bf16[32768,256]{0,1:T(8,128)(2,1)} %bitcast.97), kind=kOutput, calls=%fused_computation.10 | convolution fusion | flops 4295032832 | bytes 17039360 | tf_op jit(solution)/shard_map/snm,snk->smk/dot_general | solution.py:38
  558.3 0.0 all-reduce.3.cloned.1.call-update
  558.4 32.1 %all-reduce.3.cloned.1.call-done = f32[1,256,256]{1,2,0:T(8,128)} async-done(((f32[1,256,256]{1,2,0:T(8,128)}), f32[1,256,256]{1,2,0:T(8,128)}) %all-reduce.3.cloned.1.call-update) | async-done | bytes 262160 | tf_op jit(solution)/shard_map/psum | solution.py:41
  590.5 1.1 copy.24
  591.6 1.0 fusion.9
  592.6 11.7 %custom-call.17 = f32[1,128,128]{2,1,0:T(8,128)S(1)} custom-call(f32[1,128,128]{2,1,0:T(8,128)S(1)} %cholesky.117), custom_call_target="Cholesky" | custom-call | tf_op jit(solution)/shard_map/jit(cholesky)/cholesky | solution.py:41
  604.3 9.8 %custom-call.18 = f32[1,1,128,128]{2,3,1,0:T(8,128)S(1)} custom-call(f32[1,1,128,128]{3,2,1,0:T(8,128)S(1)} %get-tuple-element.25), custom_call_target="InvertDiagBlocksLowerTriangular" | custom-call | tf_op jit(solution)/shard_map/jit(cholesky)/cholesky | solution.py:41
  614.2 0.2 bitcast_dynamic-update-slice_fusion.1
  614.4 0.3 fusion.7
  614.7 11.9 %custom-call.19 = f32[1,128,128]{2,1,0:T(8,128)S(1)} custom-call(f32[1,128,128]{2,1,0:T(8,128)S(1)} %fusion.7), custom_call_target="Cholesky" | custom-call | tf_op jit(solution)/shard_map/jit(cholesky)/cholesky | solution.py:41
  626.6 0.7 compare_reduce_fusion
  628.6 0.7 bitcast_select_fusion
  629.3 0.1 triangular_solve.63
  629.4 4.0 while.1
  629.4 0.6 fusion.30
  630.0 1.3 bitcast_dynamic-update-slice_fusion.3
  631.4 0.6 fusion.30
  632.0 1.3 bitcast_dynamic-update-slice_fusion.3
  633.3 19.7 %custom-call.20 = f32[2,128,128]{1,2,0:T(8,128)S(1)} custom-call(f32[2,128,128]{2,1,0:T(8,128)S(1)} %get-tuple-element.9), custom_call_target="InvertDiagBlocksLowerTriangular" | custom-call | tf_op jit(solution)/shard_map/jit(_solve_triangular)/triangular_solve | solution.py:43
  653.0 0.3 fusion.20
  653.3 0.3 convolution_subtract_fusion
  653.6 0.3 convolution_convert_fusion.1
  653.9 0.0 copy-start.1
  653.9 12.0 %convolution_convert_fusion = bf16[32768,256]{1,0:T(8,128)(2,1)} fusion(bf16[32768,256]{0,1:T(8,128)(2,1)} %bitcast.98, bf16[128,256]{1,0:T(8,128)(2,1)S(1)} %convolution_convert_fusion.1, bf16[128,256]{1,0:T(8,128)(2,1)S(1)} %get-tuple-element.28), kind=kOutput, calls=%fused_computation.2 | convolution fusion | flops 4303618048 | bytes 33685504 | tf_op jit(solution)/shard_map/snm,smk->snk/dot_general | solution.py:45
  665.9 0.0 copy-done.1
  (9 shorter events, 0.1 us)
Async XLA Ops:
  7.2 273.8 %copy-start = (bf16[512,512]{1,0:T(8,128)(2,1)S(1)}, bf16[512,512]{1,0:T(8,128)(2,1)}, u32[]{:S(2)}) copy-start(bf16[512,512]{1,0:T(8,128)(2,1)} %param.6) | copy-start | bytes 1572868
  37.1 7.2 %copy-start.2 = (bf16[1,1,128,256]{3,2,1,0:T(8,128)(2,1)S(1)}, bf16[1,1,128,256]{3,2,1,0:T(8,128)(2,1)}, u32[]{:S(2)}) copy-start(bf16[1,1,128,256]{3,2,1,0:T(8,128)(2,1)} %param.5) | copy-start | bytes 196612
  37.1 193.1 %all-to-all-start = ((bf16[1,128,256,256]{2,1,0,3:T(8,128)(2,1)}), bf16[1,128,256,256]{2,1,0,3:T(8,128)(2,1)}, u32[]{:S(2)}, u32[]{:S(2)}) async-start(bf16[1,128,256,256]{2,1,0,3:T(8,128)(2,1)} %copy.19), calls=%async_computation | async-start | bytes 33554432 | tf_op jit(solution)/shard_map/all_to_all | solution.py:30
  44.3 546.2 %all-reduce.3.cloned.1.call-start = ((), (), s32[]{:S(2)}) async-start(), calls=%async_computation.2 | async-start | bytes 524288 | tf_op jit(solution)/shard_map/psum | solution.py:41
  653.9 12.0 %copy-start.1 = (bf16[512,512]{1,0:T(8,128)(2,1)S(1)}, bf16[512,512]{1,0:T(8,128)(2,1)}, u32[]{:S(2)}) copy-start(bf16[512,512]{1,0:T(8,128)(2,1)} %param.6) | copy-start | bytes 1572868
Sparse Core Ops, SparseCore 0:
  558.5 31.9 all-reduce.2
where the time goes:
time: 677 us; the launch traced here: 673 us
  blocking collectives  372 us (55%)
  local copies, waits for them, and re-layouts  130 us (19%)
  matrix products  59.4 us (9%)
  other arithmetic  55.7 us (8%)
  waiting for transfers between devices  32.1 us (5%)
  between operations  15.5 us (2%)
  starting transfers between devices  7.16 us (1%)
    all_to_all x1, blocking collectives, per_device(): lax.all_to_all(moved, 'site', split_axis=1, concat_axis=3, tiled=True)  187 us
    all_gather x1, blocking collectives, per_device(): every_field = lax.all_gather(fields, 'site', axis=2, tiled=True)  186 us
    another operation x6, other arithmetic, per_device(): lower = jnp.linalg.cholesky(lax.psum(local_gram, 'site'))  34.2 us
    psum x1, waiting for transfers between devices, per_device(): lower = jnp.linalg.cholesky(lax.psum(local_gram, 'site'))  32.1 us
    another operation x7, local copies, waits for them, and re-layouts  28.8 us
    all_to_all x1, local copies, waits for them, and re-layouts, per_device(): lax.all_to_all(apply_y(current, kinetic_y), 'site', split_axis=3, concat_...  25.8 us
    convert_element_type x1, local copies, waits for them, and re-layouts, scale_sites(): (factor[..., None] * current.astype(jnp.float32)).astype(jnp.bfloat16)  23.4 us
    all_to_all x1, local copies, waits for them, and re-layouts, per_device(): lax.all_to_all(moved, 'site', split_axis=1, concat_axis=3, tiled=True)  21.7 us
  transfers between devices with their start and end apart: 2, of which 1 were waited for; matrix products, arithmetic and copies ran while one was open for 0% of the time, Pallas kernels for 0%

commit v1 on v0

v1 whole, which is shorter than its diff:
```python
import functools

import jax
import jax.numpy as jnp
from jax import lax
from jax.experimental import pallas as pl
from jax.experimental.pallas import tpu as pltpu
from jax.sharding import PartitionSpec as P

ROWS = 16
LANES = 128
VMEM_LIMIT = 48 * 1024 * 1024


def partner(device, step, count):
    if count & (count - 1) == 0:
        return device ^ step
    return (step - device + count) % count


def trade(piece, step, count):
    if step == 0 and count & (count - 1) == 0:
        return piece
    return lax.ppermute(piece, "site", [(i, partner(i, step, count)) for i in range(count)])


def params():
    return pltpu.CompilerParams(vmem_limit_bytes=VMEM_LIMIT)


def y_kernel(count, chunks, band, part, walkers, kinetic, *rest):
    outs, own, turned = rest[:-2], rest[-2], rest[-1]
    me = lax.axis_index("site")
    depth = len(chunks) * count * part

    @pl.when(pl.program_id(0) == 0)
    def _():
        for i, c in enumerate(chunks):
            for s in range(count):
                start = pl.multiple_of(partner(me, s, count) * band + c * part, ROWS)
                own[pl.ds((i * count + s) * part, part), :] = kinetic[pl.ds(start, part), :]

    for r in range(ROWS):
        line = jnp.dot(own[...], walkers[r], preferred_element_type=jnp.float32)
        for h in range(turned.shape[0]):
            turned[h, pl.ds(r, depth, stride=ROWS), :] = line[:, h * LANES : (h + 1) * LANES]
    for k, out in enumerate(outs):
        for h in range(turned.shape[0]):
            piece = turned[h, pl.ds(k * part * ROWS, part * ROWS), :].astype(out.dtype)
            out[:, :, h * LANES : (h + 1) * LANES] = piece.reshape(part, ROWS, LANES)


def apply_y(walkers, kinetic_y, count, chunks, part):
    lines, width, orbitals = walkers.shape
    band = width // count
    pieces = len(chunks) * count
    depth = pieces * part
    return pl.pallas_call(
        functools.partial(y_kernel, count, chunks, band, part),
        grid=(lines // ROWS,),
        in_specs=[
            pl.BlockSpec((ROWS, width, orbitals), lambda i: (i, 0, 0)),
            pl.BlockSpec((width, width), lambda i: (0, 0)),
        ],
        out_specs=[pl.BlockSpec((part, ROWS, orbitals), lambda i: (0, i, 0))] * pieces,
        out_shape=[jax.ShapeDtypeStruct((part, lines, orbitals), jnp.bfloat16)] * pieces,
        scratch_shapes=[
            pltpu.VMEM((depth, width), jnp.bfloat16),
            pltpu.VMEM((orbitals // LANES, depth * ROWS, LANES), jnp.float32),
        ],
        compiler_params=params(),
        cost_estimate=pl.CostEstimate(
            flops=2 * depth * width * lines * orbitals,
            bytes_accessed=2 * lines * orbitals * (width + depth),
            transcendentals=0,
        ),
    )(walkers, kinetic_y)


def x_kernel(count, group, *refs):
    pieces, (field, kinetic, before) = refs[:count], refs[count : count + 3]
    outs, gram = refs[count + 3 : 2 * count + 3], refs[-1]

    @pl.when(pl.program_id(0) == 0)
    def _():
        gram[...] = before[...]

    factor = jnp.exp(field[0].astype(jnp.float32))
    total = jnp.zeros(gram.shape, jnp.float32)
    for j in range(group):
        lines = jnp.concatenate([piece[j] for piece in pieces], axis=0)
        moved = jnp.dot(kinetic[...], lines, preferred_element_type=jnp.float32)
        moved = moved.astype(jnp.bfloat16).astype(jnp.float32)
        scaled = (factor[:, j : j + 1] * moved).astype(jnp.bfloat16)
        block = scaled.shape[0] // count
        for t in range(count):
            outs[t][j] = scaled[t * block : (t + 1) * block]
        total += lax.dot_general(
            scaled, scaled, (((0,), (0,)), ((), ())), preferred_element_type=jnp.float32
        )
    gram[...] += total


def apply_x(pieces, fields, kinetic_x, gram):
    count = len(pieces)
    part, lines, orbitals = pieces[0].shape
    length = count * lines
    group = fields.shape[2]
    piece = pl.BlockSpec((group, lines, orbitals), lambda i: (i, 0, 0))
    square = pl.BlockSpec((orbitals, orbitals), lambda i: (0, 0))
    results = pl.pallas_call(
        functools.partial(x_kernel, count, group),
        grid=(part // group,),
        in_specs=[piece] * count
        + [
            pl.BlockSpec((1, length, group), lambda i: (i, 0, 0)),
            pl.BlockSpec((length, length), lambda i: (0, 0)),
            square,
        ],
        out_specs=[piece] * count + [square],
        out_shape=[jax.ShapeDtypeStruct(pieces[0].shape, jnp.bfloat16)] * count
        + [jax.ShapeDtypeStruct((orbitals, orbitals), jnp.float32)],
        compiler_params=params(),
        cost_estimate=pl.CostEstimate(
            flops=2 * part * length * orbitals * (length + orbitals),
            bytes_accessed=4 * part * length * orbitals,
            transcendentals=part * length,
        ),
    )(*pieces, fields, kinetic_x, gram)
    return results[:count], results[count]


def last_kernel(where, piece, inverse, *rest):
    out, turned = rest[-2], rest[-1]
    part, rows, orbitals = piece.shape
    product = jnp.dot(
        piece[...].reshape(part * rows, orbitals),
        inverse[...],
        preferred_element_type=jnp.float32,
    )
    for h in range(turned.shape[0]):
        turned[h] = product[:, h * LANES : (h + 1) * LANES]
        for r in range(rows):
            line = turned[h, pl.ds(r, part, stride=rows), :]
            out[r, :, h * LANES : (h + 1) * LANES] = line.astype(out.dtype)


def finish(result, piece, inverse, place, width):
    part, lines, orbitals = piece.shape
    begun = result is not None
    return pl.pallas_call(
        last_kernel,
        grid_spec=pltpu.PrefetchScalarGridSpec(
            num_scalar_prefetch=1,
            grid=(lines // ROWS,),
            in_specs=[
                pl.BlockSpec((part, ROWS, orbitals), lambda i, where: (0, i, 0)),
                pl.BlockSpec((orbitals, orbitals), lambda i, where: (0, 0)),
            ]
            + [pl.BlockSpec(memory_space=pl.ANY)] * begun,
            out_specs=pl.BlockSpec((ROWS, part, orbitals), lambda i, where: (i, where[0], 0)),
            scratch_shapes=[pltpu.VMEM((orbitals // LANES, part * ROWS, LANES), jnp.float32)],
        ),
        out_shape=jax.ShapeDtypeStruct((lines, width, orbitals), jnp.bfloat16),
        input_output_aliases={3: 0} if begun else {},
        compiler_params=params(),
        cost_estimate=pl.CostEstimate(
            flops=2 * part * lines * orbitals * orbitals,
            bytes_accessed=4 * part * lines * orbitals,
            transcendentals=0,
        ),
    )(place.reshape(1), piece, inverse, *([result] if begun else []))


def one_determinant(walkers, fields, kinetic_x, kinetic_y, count):
    lines, width, orbitals = walkers.shape
    me = lax.axis_index("site")
    band = width // count
    part = ROWS if band % ROWS == 0 else band
    chunks = band // part
    group = 8 if part % 8 == 0 else part
    steps = range(count)

    order = jnp.stack([partner(me, s, count) for s in steps])
    first = apply_y(walkers, kinetic_y, count, (0,), part)
    sent = [[trade(first[s], s, count) for s in steps]]
    if chunks > 1:
        more = apply_y(walkers, kinetic_y, count, tuple(range(1, chunks)), part)
        for c in range(1, chunks):
            sent.append([trade(more[(c - 1) * count + s], s, count) for s in steps])

    by_band = jnp.take(fields.reshape(lines, count, band), order, axis=1)
    own_fields = jnp.stack([trade(by_band[:, s], s, count) for s in steps])
    own_fields = own_fields.reshape(count * lines, band // group, group).swapaxes(0, 1)
    turned_x = kinetic_x.reshape(count, lines, count, lines)
    turned_x = jnp.take(jnp.take(turned_x, order, axis=0), order, axis=2).reshape(kinetic_x.shape)

    gram = jnp.zeros((orbitals, orbitals), jnp.float32)
    back = []
    per = part // group
    for c in range(chunks):
        pieces, gram = apply_x(sent[c], own_fields[c * per : (c + 1) * per], turned_x, gram)
        back.append([trade(pieces[s], s, count) for s in steps])

    gram = lax.psum(gram, "site") * (1.0 / (count * lines * width))
    lower = jnp.linalg.cholesky(gram)
    inverse = jax.scipy.linalg.solve_triangular(
        lower, jnp.eye(orbitals, dtype=jnp.float32), lower=True
    ).T.astype(jnp.bfloat16)

    result = None
    for c in range(chunks):
        for s in steps:
            result = finish(result, back[c][s], inverse, order[s] * chunks + c, width)
    return result, lower


def per_device(count, walkers, fields, kinetic_x, kinetic_y):
    results = [
        one_determinant(walkers[i], fields[i, 0], kinetic_x, kinetic_y, count)
        for i in range(walkers.shape[0])
    ]
    return tuple(jnp.stack(part) for part in zip(*results))


def solution(mesh):
    placed = (
        P(("grp", "spin"), "site", None, None),
        P(("grp", "spin"), None, "site", None),
        P(),
        P(),
    )
    return jax.shard_map(
        functools.partial(per_device, mesh.shape["site"]),
        mesh=mesh,
        in_specs=placed,
        out_specs=(P(("grp", "spin"), "site", None, None), P(("grp", "spin"), None, None)),
        check_vma=False,
    )
```

time: 677 us -> 439 us (0.65)
  blocking collectives: 372 us -> 0 us
  Pallas kernels: 0 us -> 144 us
  waiting for transfers between devices: 32.1 us -> 149 us
  local copies, waits for them, and re-layouts: 130 us -> 37.1 us
  matrix products: 59.4 us -> 5.49 us
  starting transfers between devices: 7.16 us -> 23.4 us
    all_to_all x1 -> x0, blocking collectives: 187 us -> none  [per_device(): lax.all_to_all(moved, 'site', split_axis=1, concat_axis=3, tiled=True)]
    all_gather x1 -> x0, blocking collectives: 186 us -> none  [per_device(): every_field = lax.all_gather(fields, 'site', axis=2, tiled=True)]
    pallas_call x0 -> x22, Pallas kernels: none -> 144 us  [the longest x16 90.4 us: finish(): pl.pallas_call(last_kernel, grid_spec=pltpu.PrefetchScalarGridSpec(num_sc...]
    ppermute x0 -> x27, waiting for transfers between devices: none -> 120 us  [trade(): lax.ppermute(piece, 'site', [(i, partner(i, step, count)) for i in range(...]
    dot_general x4 -> x0, matrix products: 58.1 us -> none  [the longest x1 18.3 us: apply_x(): jnp.einsum('xz,szym->sxym', kinetic_x, current, preferred_element_type=jn...]
    all_to_all x2 -> x0, local copies, waits for them, and re-layouts: 47.5 us -> none  [the longest x1 25.8 us: per_device(): lax.all_to_all(apply_y(current, kinetic_y), 'site', split_axis=3, concat_...]
    convert_element_type x2 -> x0, local copies, waits for them, and re-layouts: 41.3 us -> none  [the longest x1 23.4 us: scale_sites(): (factor[..., None] * current.astype(jnp.float32)).astype(jnp.bfloat16)]
    ppermute x0 -> x27, starting transfers between devices: none -> 23.4 us  [trade(): lax.ppermute(piece, 'site', [(i, partner(i, step, count)) for i in range(...]
  transfers between devices with their start and end apart: 2 -> 28, of which waited for: 1 -> 8; matrix products, arithmetic and copies ran while one was open for 0% -> 19% of each run, Pallas kernels for 0% -> 27%
where the time goes in v1:
time: 439 us; the launch traced here: 436 us
  waiting for transfers between devices  149 us (34%)
  Pallas kernels  144 us (33%)
  other arithmetic  62.4 us (14%)
  local copies, waits for them, and re-layouts  37.1 us (8%)
  starting transfers between devices  23.4 us (5%)
  between operations  15.6 us (4%)
  matrix products  5.49 us (1%)
    ppermute x27, waiting for transfers between devices, trade(): lax.ppermute(piece, 'site', [(i, partner(i, step, count)) for i in range(...  120 us
    pallas_call x16, Pallas kernels, finish(): pl.pallas_call(last_kernel, grid_spec=pltpu.PrefetchScalarGridSpec(num_sc...  90.4 us
    another operation x6, other arithmetic, one_determinant(): lower = jnp.linalg.cholesky(gram)  34 us
    psum x1, waiting for transfers between devices, one_determinant(): gram = lax.psum(gram, 'site') * (1.0 / (count * lines * width))  29 us
    pallas_call x2, Pallas kernels, apply_y(): pl.pallas_call(functools.partial(y_kernel, count, chunks, band, part), gr...  28.2 us
    pallas_call x4, Pallas kernels, apply_x(): pl.pallas_call(functools.partial(x_kernel, count, group), grid=(part // g...  25.1 us
    ppermute x27, starting transfers between devices, trade(): lax.ppermute(piece, 'site', [(i, partner(i, step, count)) for i in range(...  23.4 us
    another operation x2, other arithmetic, one_determinant(): jax.scipy.linalg.solve_triangular(lower, jnp.eye(orbitals, dtype=jnp.floa...  21.1 us
  transfers between devices with their start and end apart: 28, of which 8 were waited for; matrix products, arithmetic and copies ran while one was open for 19% of the time, Pallas kernels for 27%

profile of v1, /device:TPU:1, one launch (start us, length us, event | category | flops | bytes accessed | tf_op | source)
XLA Modules:
  0.0 436.5 jit_solution(352249947053446896)
XLA Ops:
  8.1 11.7 %shard_map.60 = (bf16[16,128,256]{2,1,0:T(8,128)(2,1)S(1)}, bf16[16,128,256]{2,1,0:T(8,128)(2,1)}, bf16[16,128,256]{2,1,0:T(8,128)(2,1)}, bf16[16,128,256]{2,1,0:T(8,128)(2,1)}) custom-call(bf16[128,256,256]{2,1,0:T(8,128)(2,1)} %bitcast.88, bf16[256,256]{1,0:T(8,128)(2,1)S(1)} %copy-done.2), custom_call_target="tpu_custom_call" | custom-call | flops 1073741824 | bytes 20971520 | tf_op jit(solution)/shard_map/pallas_call | solution.py:58
  20.9 2.7 collective-permute-start.13
  23.6 16.5 %shard_map.59 = (bf16[16,128,256]{2,1,0:T(8,128)(2,1)S(1)}, bf16[16,128,256]{2,1,0:T(8,128)(2,1)S(1)}, bf16[16,128,256]{2,1,0:T(8,128)(2,1)}, bf16[16,128,256]{2...) custom-call(bf16[128,256,256]{2,1,0:T(8,128)(2,1)} %bitcast.89, ...), custom_call_target="tpu_custom_call" | custom-call | flops 3221225472 | bytes 29360128 | tf_op jit(solution)/shard_map/pallas_call | solution.py:58
  42.0 1.6 collective-permute-start.10
  46.0 46.7 %collective-permute-done.4 = bf16[128,64]{0,1:T(8,128)(2,1)S(1)} collective-permute-done((bf16[128,64]{0,1:T(8,128)(2,1)S(1)}, bf16[128,64]{0,1:T(8,128)(2,1)S(1)}, u32[]{:S(2)}, u32[]{:S(2)}) %collective-permute-start.4) | collective-permute-done | bytes 16416 | tf_op jit(solution)/shard_map/ppermute | solution.py:24
  92.7 1.8 collective-permute-start.5
  94.5 1.4 collective-permute-done.5
  95.9 1.9 collective-permute-start.11
  104.4 1.4 copy.48
  106.0 1.7 collective-permute-start.8
  109.2 12.6 %collective-permute-done.11.refs_3_ = bf16[16,128,256]{2,1,0:T(8,128)(2,1)} collective-permute-done((bf16[16,128,256]{2,1,0:T(8,128)(2,1)}, bf16[16,128,256]{2,1,0:T(8,128)(2,1)}, u32[]{:S(2)}, u32[]{:S(2)}) %collective-permute-start.11) | collective-permute-done | bytes 1048608 | tf_op jit(solution)/shard_map/ppermute | solution.py:24
  121.8 1.6 collective-permute-start.1
  125.2 6.2 %shard_map.61 = (bf16[16,128,256]{2,1,0:T(8,128)(2,1)S(1)}, bf16[16,128,256]{2,1,0:T(8,128)(2,1)S(1)}, bf16[16,128,256]{2,1,0:T(8,128)(2,1)S(1)}, bf16[16,128,256]{2,1,0:T(8,128)(2,1)S(1)}, f32[256,256]{1,0:T(8,128)S(1)}) custom-call(bf16[16,128,256]{2,1,0:T(8,128)(2,1)} %copy-done.16, bf16[16,128,256]{2,1,0:T(8,128)(2,1)} %collective-permute-done.12.refs_1_, ...), custom_call_target="tpu_custom_call" | custom-call | flops 3221225472 | bytes 8388608 | tf_op jit(solution)/shard_map/pallas_call | solution.py:111
  134.4 6.5 %shard_map.62 = (bf16[16,128,256]{2,1,0:T(8,128)(2,1)S(1)}, bf16[16,128,256]{2,1,0:T(8,128)(2,1)S(1)}, bf16[16,128,256]{2,1,0:T(8,128)(2,1)S(1)}, bf16[16,128,256]{2,1,0:T(8,128)(2,1)S(1)}, f32[256,256]{1,0:T(8,128)S(1)}) custom-call(bf16[16,128,256]{2,1,0:T(8,128)(2,1)} %copy-done.17, bf16[16,128,256]{2,1,0:T(8,128)(2,1)} %collective-permute-done.9.refs_1_, ...), custom_call_target="tpu_custom_call" | custom-call | flops 3221225472 | bytes 8388608 | tf_op jit(solution)/shard_map/pallas_call | solution.py:111
  144.0 22.8 %collective-permute-done.8.refs_3_ = bf16[16,128,256]{2,1,0:T(8,128)(2,1)} collective-permute-done((bf16[16,128,256]{2,1,0:T(8,128)(2,1)}, bf16[16,128,256]{2,1,0:T(8,128)(2,1)}, u32[]{:S(2)}, u32[]{:S(2)}) %collective-permute-start.8) | collective-permute-done | bytes 1048608 | tf_op jit(solution)/shard_map/ppermute | solution.py:24
  166.7 6.2 %shard_map.63 = (bf16[16,128,256]{2,1,0:T(8,128)(2,1)S(1)}, bf16[16,128,256]{2,1,0:T(8,128)(2,1)S(1)}, bf16[16,128,256]{2,1,0:T(8,128)(2,1)S(1)}, bf16[16,128,256]{2,1,0:T(8,128)(2,1)S(1)}, f32[256,256]{1,0:T(8,128)S(1)}) custom-call(bf16[16,128,256]{2,1,0:T(8,128)(2,1)} %copy-done.15, bf16[16,128,256]{2,1,0:T(8,128)(2,1)} %collective-permute-done.6.refs_1_, ...), custom_call_target="tpu_custom_call" | custom-call | flops 3221225472 | bytes 8388608 | tf_op jit(solution)/shard_map/pallas_call | solution.py:111
  175.9 12.7 %collective-permute-done.1.refs_2_ = bf16[16,128,256]{2,1,0:T(8,128)(2,1)S(1)} collective-permute-done((bf16[16,128,256]{2,1,0:T(8,128)(2,1)}, bf16[16,128,256]{2,1,0:T(8,128)(2,1)S(1)}, u32[]{:S(2)}, u32[]{:S(2)}) %collective-permute-start.1) | collective-permute-done | bytes 1048608 | tf_op jit(solution)/shard_map/ppermute | solution.py:24
  188.6 22.6 %collective-permute-done.2.refs_3_ = bf16[16,128,256]{2,1,0:T(8,128)(2,1)S(1)} collective-permute-done((bf16[16,128,256]{2,1,0:T(8,128)(2,1)}, bf16[16,128,256]{2,1,0:T(8,128)(2,1)S(1)}, u32[]{:S(2)}, u32[]{:S(2)}) %collective-permute-start.2) | collective-permute-done | bytes 1048608 | tf_op jit(solution)/shard_map/ppermute | solution.py:24
  213.2 6.2 %shard_map.64 = (bf16[16,128,256]{2,1,0:T(8,128)(2,1)S(1)}, bf16[16,128,256]{2,1,0:T(8,128)(2,1)S(1)}, bf16[16,128,256]{2,1,0:T(8,128)(2,1)S(1)}, bf16[16,128,256]{2,1,0:T(8,128)(2,1)S(1)}, f32[256,256]{1,0:T(8,128)S(1)}) custom-call(bf16[16,128,256]{2,1,0:T(8,128)(2,1)} %get-tuple-element.38.refs_0_, bf16[16,128,256]{2,1,0:T(8,128)(2,1)} %copy-done.25, ...), custom_call_target="tpu_custom_call" | custom-call | flops 3221225472 | bytes 8388608 | tf_op jit(solution)/shard_map/pallas_call | solution.py:111
  224.2 1.7 collective-permute-start.25
  226.4 1.4 collective-permute-start.22
  227.8 29.0 %all-reduce.3.cloned.1.call-done = f32[256,256]{0,1:T(8,128)} async-done(((f32[256,256]{0,1:T(8,128)}), f32[256,256]{0,1:T(8,128)}) %all-reduce.3.cloned.1.call-update) | async-done | bytes 262160 | tf_op jit(solution)/shard_map/psum | solution.py:205
  256.8 1.7 broadcast_multiply_fusion
  261.3 11.7 %cholesky.49 = f32[128,128]{1,0:T(8,128)S(1)} custom-call(f32[128,128]{1,0:T(8,128)S(1)} %cholesky.115), custom_call_target="Cholesky" | custom-call | tf_op jit(solution)/shard_map/jit(cholesky)/cholesky | solution.py:206
  273.0 9.8 %custom-call.15 = f32[1,128,128]{1,2,0:T(8,128)S(1)} custom-call(f32[1,128,128]{2,1,0:T(8,128)S(1)} %get-tuple-element.101), custom_call_target="InvertDiagBlocksLowerTriangular" | custom-call | tf_op jit(solution)/shard_map/jit(cholesky)/cholesky | solution.py:206
  285.0 11.7 %cholesky.103 = f32[128,128]{1,0:T(8,128)S(1)} custom-call(f32[128,128]{1,0:T(8,128)S(1)} %convolution_subtract_fusion.1), custom_call_target="Cholesky" | custom-call | tf_op jit(solution)/shard_map/jit(cholesky)/cholesky | solution.py:206
  296.7 2.1 collective-permute-start.21
  301.1 1.7 fusion.2
  302.8 5.0 %while.1 = (s32[]{:T(128)}, f32[256,256]{1,0:T(8,128)S(1)}, s32[2,2]{1,0:T(2,128)S(1)}, f32[2,128,128]{2,1,0:T(8,128)}, s32[]{:T(128)}) while((s32[]{:T(128)}, f32[256,256]{1,0:T(8,128)S(1)}, s32[2,2]{1,0:T(2,128)S(1)}, f32[2,128,128]{2,1,0:T(8,128)}, s32[]{:T(128)}) %tuple.34), condition=%wide.while_cond, body=%wide.while_body.sunk | while | flops 2 | bytes 132705 | solution.py:207
  303.4 1.9 bitcast_dynamic-update-slice_fusion.2
  305.9 1.9 bitcast_dynamic-update-slice_fusion.2
  307.8 21.1 %custom-call.16 = f32[2,128,128]{1,2,0:T(8,128)} custom-call(f32[2,128,128]{2,1,0:T(8,128)} %get-tuple-element.81), custom_call_target="InvertDiagBlocksLowerTriangular" | custom-call | tf_op jit(solution)/shard_map/jit(_solve_triangular)/triangular_solve | solution.py:207
  339.2 4.1 shard_map.65.rest_0_
  343.2 6.2 %shard_map.66.rest_0_ = bf16[128,256,256]{2,1,0:T(8,128)(2,1)} custom-call(s32[1]{0:T(128)} %bitcast.42.where, bf16[16,128,256]{2,1,0:T(8,128)(2,1)} %collective-permute-done.26.piece, bf16[256,256]{1,0:T(8,128)(2,1)S(1)} %maximum_bitcast_fusion.inverse, bf16[128,256,256]{2,1,0:T(8,128)(2,1)} %shard_map.65.rest_0_), custom_call_target="tpu_custom_call", output_to_operand_aliasing={{}: (3, {})} | custom-call | flops 268435456 | bytes 2097152 | tf_op jit(solution)/shard_map/pallas_call | solution.py:151
  349.4 6.2 %shard_map.67.rest_0_ = bf16[128,256,256]{2,1,0:T(8,128)(2,1)} custom-call(s32[1]{0:T(128)} %bitcast.41.where, bf16[16,128,256]{2,1,0:T(8,128)(2,1)} %collective-permute-done.25.piece, bf16[256,256]{1,0:T(8,128)(2,1)S(1)} %maximum_bitcast_fusion.inverse, bf16[128,256,256]{2,1,0:T(8,128)(2,1)} %shard_map.66.rest_0_), custom_call_target="tpu_custom_call", output_to_operand_aliasing={{}: (3, {})} | custom-call | flops 268435456 | bytes 2097152 | tf_op jit(solution)/shard_map/pallas_call | solution.py:151
  355.6 6.2 %shard_map.68.rest_0_ = bf16[128,256,256]{2,1,0:T(8,128)(2,1)} custom-call(s32[1]{0:T(128)} %bitcast.40.where, bf16[16,128,256]{2,1,0:T(8,128)(2,1)} %collective-permute-done.24.piece, bf16[256,256]{1,0:T(8,128)(2,1)S(1)} %maximum_bitcast_fusion.inverse, bf16[128,256,256]{2,1,0:T(8,128)(2,1)} %shard_map.67.rest_0_), custom_call_target="tpu_custom_call", output_to_operand_aliasing={{}: (3, {})} | custom-call | flops 268435456 | bytes 2097152 | tf_op jit(solution)/shard_map/pallas_call | solution.py:151
  361.8 4.0 shard_map.69.rest_0_
  365.8 6.2 %shard_map.70.rest_0_ = bf16[128,256,256]{2,1,0:T(8,128)(2,1)} custom-call(s32[1]{0:T(128)} %bitcast.38.where, bf16[16,128,256]{2,1,0:T(8,128)(2,1)} %collective-permute-done.23.piece, bf16[256,256]{1,0:T(8,128)(2,1)S(1)} %maximum_bitcast_fusion.inverse, bf16[128,256,256]{2,1,0:T(8,128)(2,1)} %shard_map.69.rest_0_), custom_call_target="tpu_custom_call", output_to_operand_aliasing={{}: (3, {})} | custom-call | flops 268435456 | bytes 2097152 | tf_op jit(solution)/shard_map/pallas_call | solution.py:151
  372.0 6.2 %shard_map.71.rest_0_ = bf16[128,256,256]{2,1,0:T(8,128)(2,1)} custom-call(s32[1]{0:T(128)} %bitcast.37.where, bf16[16,128,256]{2,1,0:T(8,128)(2,1)} %collective-permute-done.22.piece, bf16[256,256]{1,0:T(8,128)(2,1)S(1)} %maximum_bitcast_fusion.inverse, bf16[128,256,256]{2,1,0:T(8,128)(2,1)} %shard_map.70.rest_0_), custom_call_target="tpu_custom_call", output_to_operand_aliasing={{}: (3, {})} | custom-call | flops 268435456 | bytes 2097152 | tf_op jit(solution)/shard_map/pallas_call | solution.py:151
  378.2 6.2 %shard_map.72.rest_0_ = bf16[128,256,256]{2,1,0:T(8,128)(2,1)} custom-call(s32[1]{0:T(128)} %bitcast.36.where, bf16[16,128,256]{2,1,0:T(8,128)(2,1)} %collective-permute-done.21.piece, bf16[256,256]{1,0:T(8,128)(2,1)S(1)} %maximum_bitcast_fusion.inverse, bf16[128,256,256]{2,1,0:T(8,128)(2,1)} %shard_map.71.rest_0_), custom_call_target="tpu_custom_call", output_to_operand_aliasing={{}: (3, {})} | custom-call | flops 268435456 | bytes 2097152 | tf_op jit(solution)/shard_map/pallas_call | solution.py:151
  384.4 4.1 shard_map.73.rest_0_
  388.4 6.2 %shard_map.74.rest_0_ = bf16[128,256,256]{2,1,0:T(8,128)(2,1)} custom-call(s32[1]{0:T(128)} %bitcast.34.where, bf16[16,128,256]{2,1,0:T(8,128)(2,1)} %collective-permute-done.20.piece, bf16[256,256]{1,0:T(8,128)(2,1)S(1)} %maximum_bitcast_fusion.inverse, bf16[128,256,256]{2,1,0:T(8,128)(2,1)} %shard_map.73.rest_0_), custom_call_target="tpu_custom_call", output_to_operand_aliasing={{}: (3, {})} | custom-call | flops 268435456 | bytes 2097152 | tf_op jit(solution)/shard_map/pallas_call | solution.py:151
  394.6 6.2 %shard_map.75.rest_0_ = bf16[128,256,256]{2,1,0:T(8,128)(2,1)} custom-call(s32[1]{0:T(128)} %bitcast.33.where, bf16[16,128,256]{2,1,0:T(8,128)(2,1)} %collective-permute-done.19.piece, bf16[256,256]{1,0:T(8,128)(2,1)S(1)} %maximum_bitcast_fusion.inverse, bf16[128,256,256]{2,1,0:T(8,128)(2,1)} %shard_map.74.rest_0_), custom_call_target="tpu_custom_call", output_to_operand_aliasing={{}: (3, {})} | custom-call | flops 268435456 | bytes 2097152 | tf_op jit(solution)/shard_map/pallas_call | solution.py:151
  400.8 6.2 %shard_map.76.rest_0_ = bf16[128,256,256]{2,1,0:T(8,128)(2,1)} custom-call(s32[1]{0:T(128)} %bitcast.32.where, bf16[16,128,256]{2,1,0:T(8,128)(2,1)} %collective-permute-done.18.piece, bf16[256,256]{1,0:T(8,128)(2,1)S(1)} %maximum_bitcast_fusion.inverse, bf16[128,256,256]{2,1,0:T(8,128)(2,1)} %shard_map.75.rest_0_), custom_call_target="tpu_custom_call", output_to_operand_aliasing={{}: (3, {})} | custom-call | flops 268435456 | bytes 2097152 | tf_op jit(solution)/shard_map/pallas_call | solution.py:151
  407.0 4.0 shard_map.77.rest_0_
  411.1 6.2 %shard_map.78.rest_0_ = bf16[128,256,256]{2,1,0:T(8,128)(2,1)} custom-call(s32[1]{0:T(128)} %bitcast.30.where, bf16[16,128,256]{2,1,0:T(8,128)(2,1)} %collective-permute-done.17.piece, bf16[256,256]{1,0:T(8,128)(2,1)S(1)} %maximum_bitcast_fusion.inverse, bf16[128,256,256]{2,1,0:T(8,128)(2,1)} %shard_map.77.rest_0_), custom_call_target="tpu_custom_call", output_to_operand_aliasing={{}: (3, {})} | custom-call | flops 268435456 | bytes 2097152 | tf_op jit(solution)/shard_map/pallas_call | solution.py:151
  417.3 6.2 %shard_map.79.rest_0_ = bf16[128,256,256]{2,1,0:T(8,128)(2,1)} custom-call(s32[1]{0:T(128)} %bitcast.29.where, bf16[16,128,256]{2,1,0:T(8,128)(2,1)} %collective-permute-done.16.piece, bf16[256,256]{1,0:T(8,128)(2,1)S(1)} %maximum_bitcast_fusion.inverse, bf16[128,256,256]{2,1,0:T(8,128)(2,1)} %shard_map.78.rest_0_), custom_call_target="tpu_custom_call", output_to_operand_aliasing={{}: (3, {})} | custom-call | flops 268435456 | bytes 2097152 | tf_op jit(solution)/shard_map/pallas_call | solution.py:151
  423.4 6.2 %shard_map.80 = bf16[128,256,256]{2,1,0:T(8,128)(2,1)} custom-call(s32[1]{0:T(128)} %bitcast.where, bf16[16,128,256]{2,1,0:T(8,128)(2,1)} %collective-permute-done.15.piece, bf16[256,256]{1,0:T(8,128)(2,1)S(1)} %maximum_bitcast_fusion.inverse, bf16[128,256,256]{2,1,0:T(8,128)(2,1)} %shard_map.79.rest_0_), custom_call_target="tpu_custom_call", output_to_operand_aliasing={{}: (3, {})} | custom-call | flops 268435456 | bytes 2097152 | tf_op jit(solution)/shard_map/pallas_call | solution.py:151
  (140 shorter events, 49.8 us)
Async XLA Ops:
  7.2 249.6 %all-reduce.3.cloned.1.call-start = ((), (), s32[]{:S(2)}) async-start(), calls=%async_computation | async-start | bytes 524288 | tf_op jit(solution)/shard_map/psum | solution.py:205
  8.1 35.5 %copy-start.24 = (bf16[1,1,128,256]{3,2,1,0:T(8,128)(2,1)S(1)}, bf16[1,1,128,256]{3,2,1,0:T(8,128)(2,1)}, u32[]{:S(2)}) copy-start(bf16[1,1,128,256]{3,2,1,0:T(8,128)(2,1)} %param.5) | copy-start | bytes 196612
  8.1 90.3 %copy-start.23 = (bf16[512,512]{1,0:T(8,128)(2,1)S(1)}, bf16[512,512]{1,0:T(8,128)(2,1)}, u32[]{:S(2)}) copy-start(bf16[512,512]{1,0:T(8,128)(2,1)} %param.6) | copy-start | bytes 1572868
  19.9 1.0 copy-start.16
  20.8 77.0 %collective-permute-start.12 = (bf16[16,128,256]{2,1,0:T(8,128)(2,1)}, bf16[16,128,256]{2,1,0:T(8,128)(2,1)}, u32[]{:S(2)}, u32[]{:S(2)}) collective-permute-start(bf16[16,128,256]{2,1,0:T(8,128)(2,1)} %get-tuple-element.51), channel_id=1, source_target_pairs={{0,4},{4,0},{8,12},{12,8},{1,5},{5,1},{9,13},{13,9},{2,6},{6,2},{1... | collective-permute-start | bytes 3145736 | tf_op jit(solution)/shard_map/ppermute | solution.py:24
  20.9 77.1 %collective-permute-start.13 = (bf16[16,128,256]{2,1,0:T(8,128)(2,1)}, bf16[16,128,256]{2,1,0:T(8,128)(2,1)}, u32[]{:S(2)}, u32[]{:S(2)}) collective-permute-start(bf16[16,128,256]{2,1,0:T(8,128)(2,1)} %get-tuple-element.52), channel_id=1, source_target_pairs={{0,8},{4,12},{8,0},{12,4},{1,9},{5,13},{9,1},{13,5},{2,10},{6,14},... | collective-permute-start | bytes 3145736 | tf_op jit(solution)/shard_map/ppermute | solution.py:24
  23.6 82.4 %collective-permute-start.14 = (bf16[16,128,256]{2,1,0:T(8,128)(2,1)}, bf16[16,128,256]{2,1,0:T(8,128)(2,1)}, u32[]{:S(2)}, u32[]{:S(2)}) collective-permute-start(bf16[16,128,256]{2,1,0:T(8,128)(2,1)} %get-tuple-element.53), channel_id=1, source_target_pairs={{0,12},{4,8},{8,4},{12,0},{1,13},{5,9},{9,5},{13,1},{2,14},{6,10},... | collective-permute-start | bytes 3145736 | tf_op jit(solution)/shard_map/ppermute | solution.py:24
  41.0 1.0 copy-start.20
  42.0 65.7 %copy-start.17 = (bf16[16,128,256]{2,1,0:T(8,128)(2,1)}, bf16[16,128,256]{2,1,0:T(8,128)(2,1)S(1)}, u32[]{:S(2)}) copy-start(bf16[16,128,256]{2,1,0:T(8,128)(2,1)S(1)} %get-tuple-element.46.refs_0_) | copy-start | bytes 3145732
  42.0 64.0 %collective-permute-start.10 = (bf16[16,128,256]{2,1,0:T(8,128)(2,1)}, bf16[16,128,256]{2,1,0:T(8,128)(2,1)}, u32[]{:S(2)}, u32[]{:S(2)}) collective-permute-start(bf16[16,128,256]{2,1,0:T(8,128)(2,1)} %get-tuple-element.48), channel_id=1, source_target_pairs={{0,8},{4,12},{8,0},{12,4},{1,9},{5,13},{9,1},{13,5},{2,10},{6,14},... | collective-permute-start | bytes 3145736 | tf_op jit(solution)/shard_map/ppermute | solution.py:24
  44.6 1.4 collective-permute-start.3
  46.0 46.7 %collective-permute-start.4 = (bf16[128,64]{0,1:T(8,128)(2,1)S(1)}, bf16[128,64]{0,1:T(8,128)(2,1)S(1)}, u32[]{:S(2)}, u32[]{:S(2)}) collective-permute-start(bf16[128,64]{0,1:T(8,128)(2,1)S(1)} %get-tuple-element.104), channel_id=1, source_target_pairs={{0,8},{4,12},{8,0},{12,4},{1,9},{5,13},{9,1},{13,5},{2,10},{6,14},... | collective-permute-start | bytes 49160 | tf_op jit(solution)/shard_map/ppermute | solution.py:24
  92.7 3.2 collective-permute-start.5
  95.9 25.9 %collective-permute-start.11 = (bf16[16,128,256]{2,1,0:T(8,128)(2,1)}, bf16[16,128,256]{2,1,0:T(8,128)(2,1)}, u32[]{:S(2)}, u32[]{:S(2)}) collective-permute-start(bf16[16,128,256]{2,1,0:T(8,128)(2,1)} %copy-done.20), channel_id=1, source_target_pairs={{0,12},{4,8},{8,4},{12,0},{1,13},{5,9},{9,5},{13,1},{2,14},{6,10},... | collective-permute-start | bytes 3145736 | tf_op jit(solution)/shard_map/ppermute | solution.py:24
  97.9 24.0 %collective-permute-start.9 = (bf16[16,128,256]{2,1,0:T(8,128)(2,1)S(1)}, bf16[16,128,256]{2,1,0:T(8,128)(2,1)}, u32[]{:S(2)}, u32[]{:S(2)}) collective-permute-start(bf16[16,128,256]{2,1,0:T(8,128)(2,1)S(1)} %get-tuple-element.47), channel_id=1, source_target_pairs={{0,4},{4,0},{8,12},{12,8},{1,5},{5,1},{9,13},{13,9},{2,6},{6,2},{1... | collective-permute-start | bytes 3145736 | tf_op jit(solution)/shard_map/ppermute | solution.py:24
  98.0 25.5 %collective-permute-start.6 = (bf16[16,128,256]{2,1,0:T(8,128)(2,1)}, bf16[16,128,256]{2,1,0:T(8,128)(2,1)}, u32[]{:S(2)}, u32[]{:S(2)}) collective-permute-start(bf16[16,128,256]{2,1,0:T(8,128)(2,1)} %get-tuple-element.43), channel_id=1, source_target_pairs={{0,4},{4,0},{8,12},{12,8},{1,5},{5,1},{9,13},{13,9},{2,6},{6,2},{1... | collective-permute-start | bytes 3145736 | tf_op jit(solution)/shard_map/ppermute | solution.py:24
  105.9 38.0 %collective-permute-start.7 = (bf16[16,128,256]{2,1,0:T(8,128)(2,1)}, bf16[16,128,256]{2,1,0:T(8,128)(2,1)}, u32[]{:S(2)}, u32[]{:S(2)}) collective-permute-start(bf16[16,128,256]{2,1,0:T(8,128)(2,1)} %get-tuple-element.44), channel_id=1, source_target_pairs={{0,8},{4,12},{8,0},{12,4},{1,9},{5,13},{9,1},{13,5},{2,10},{6,14},... | collective-permute-start | bytes 3145736 | tf_op jit(solution)/shard_map/ppermute | solution.py:24
  106.0 60.8 %collective-permute-start.8 = (bf16[16,128,256]{2,1,0:T(8,128)(2,1)}, bf16[16,128,256]{2,1,0:T(8,128)(2,1)}, u32[]{:S(2)}, u32[]{:S(2)}) collective-permute-start(bf16[16,128,256]{2,1,0:T(8,128)(2,1)} %get-tuple-element.45), channel_id=1, source_target_pairs={{0,12},{4,8},{8,4},{12,0},{1,13},{5,9},{9,5},{13,1},{2,14},{6,10},... | collective-permute-start | bytes 3145736 | tf_op jit(solution)/shard_map/ppermute | solution.py:24
  107.8 65.1 %copy-start.3 = (bf16[512,512]{1,0:T(8,128)(2,1)}, bf16[512,512]{1,0:T(8,128)(2,1)S(1)}, u32[]{:S(2)}) copy-start(bf16[512,512]{1,0:T(8,128)(2,1)S(1)} %bitcast_select_fusion.refs_5_) | copy-start | bytes 1572868
  121.8 54.1 %collective-permute-start = (bf16[16,128,256]{2,1,0:T(8,128)(2,1)}, bf16[16,128,256]{2,1,0:T(8,128)(2,1)S(1)}, u32[]{:S(2)}, u32[]{:S(2)}) collective-permute-start(bf16[16,128,256]{2,1,0:T(8,128)(2,1)} %get-tuple-element.39), channel_id=1, source_target_pairs={{0,4},{4,0},{8,12},{12,8},{1,5},{5,1},{9,13},{13,9},{2,6},{6,2},{1... | collective-permute-start | bytes 3145736 | tf_op jit(solution)/shard_map/ppermute | solution.py:24
  121.8 66.8 %collective-permute-start.1 = (bf16[16,128,256]{2,1,0:T(8,128)(2,1)}, bf16[16,128,256]{2,1,0:T(8,128)(2,1)S(1)}, u32[]{:S(2)}, u32[]{:S(2)}) collective-permute-start(bf16[16,128,256]{2,1,0:T(8,128)(2,1)} %get-tuple-element.40), channel_id=1, source_target_pairs={{0,8},{4,12},{8,0},{12,4},{1,9},{5,13},{9,1},{13,5},{2,10},{6,14},... | collective-permute-start | bytes 3145736 | tf_op jit(solution)/shard_map/ppermute | solution.py:24
  123.5 87.7 %collective-permute-start.2 = (bf16[16,128,256]{2,1,0:T(8,128)(2,1)}, bf16[16,128,256]{2,1,0:T(8,128)(2,1)S(1)}, u32[]{:S(2)}, u32[]{:S(2)}) collective-permute-start(bf16[16,128,256]{2,1,0:T(8,128)(2,1)} %get-tuple-element.41), channel_id=1, source_target_pairs={{0,12},{4,8},{8,4},{12,0},{1,13},{5,9},{9,5},{13,1},{2,14},{6,10},... | collective-permute-start | bytes 3145736 | tf_op jit(solution)/shard_map/ppermute | solution.py:24
  131.4 1.0 copy-start.13
  132.4 1.0 copy-start.18
  133.5 1.0 copy-start.19
  134.4 84.9 %copy-start = (bf16[16,128,256]{2,1,0:T(8,128)(2,1)}, bf16[16,128,256]{2,1,0:T(8,128)(2,1)S(1)}, u32[]{:S(2)}) copy-start(bf16[16,128,256]{2,1,0:T(8,128)(2,1)S(1)} %get-tuple-element.73.piece) | copy-start | bytes 3145732
  141.0 1.0 copy-start.10
  143.0 1.0 copy-start.14
  172.9 1.0 copy-start.6
  174.0 1.0 copy-start.8
  175.9 35.3 %copy-start.25 = (bf16[16,128,256]{2,1,0:T(8,128)(2,1)}, bf16[16,128,256]{2,1,0:T(8,128)(2,1)S(1)}, u32[]{:S(2)}) copy-start(bf16[16,128,256]{2,1,0:T(8,128)(2,1)S(1)} %collective-permute-done.refs_1_) | copy-start | bytes 3145732
  188.6 22.6 %copy-start.26 = (bf16[16,128,256]{2,1,0:T(8,128)(2,1)}, bf16[16,128,256]{2,1,0:T(8,128)(2,1)S(1)}, u32[]{:S(2)}) copy-start(bf16[16,128,256]{2,1,0:T(8,128)(2,1)S(1)} %collective-permute-done.1.refs_2_) | copy-start | bytes 3145732
  212.2 1.0 copy-start.4
  221.4 1.0 copy-start.9
  223.9 72.9 %collective-permute-start.26 = (bf16[16,128,256]{2,1,0:T(8,128)(2,1)}, bf16[16,128,256]{2,1,0:T(8,128)(2,1)}, u32[]{:S(2)}, u32[]{:S(2)}) collective-permute-start(bf16[16,128,256]{2,1,0:T(8,128)(2,1)} %copy-done.19), channel_id=1, source_target_pairs={{0,4},{4,0},{8,12},{12,8},{1,5},{5,1},{9,13},{13,9},{2,6},{6,2},{1... | collective-permute-start | bytes 3145736 | tf_op jit(solution)/shard_map/ppermute | solution.py:24
  224.2 74.7 %collective-permute-start.25 = (bf16[16,128,256]{2,1,0:T(8,128)(2,1)}, bf16[16,128,256]{2,1,0:T(8,128)(2,1)}, u32[]{:S(2)}, u32[]{:S(2)}) collective-permute-start(bf16[16,128,256]{2,1,0:T(8,128)(2,1)} %copy-done.18), channel_id=1, source_target_pairs={{0,8},{4,12},{8,0},{12,4},{1,9},{5,13},{9,1},{13,5},{2,10},{6,14},... | collective-permute-start | bytes 3145736 | tf_op jit(solution)/shard_map/ppermute | solution.py:24
  225.9 103.0 %collective-permute-start.24 = (bf16[16,128,256]{2,1,0:T(8,128)(2,1)}, bf16[16,128,256]{2,1,0:T(8,128)(2,1)}, u32[]{:S(2)}, u32[]{:S(2)}) collective-permute-start(bf16[16,128,256]{2,1,0:T(8,128)(2,1)} %copy-done.13), channel_id=1, source_target_pairs={{0,12},{4,8},{8,4},{12,0},{1,13},{5,9},{9,5},{13,1},{2,14},{6,10},... | collective-permute-start | bytes 3145736 | tf_op jit(solution)/shard_map/ppermute | solution.py:24
  226.0 104.2 %collective-permute-start.23 = (bf16[16,128,256]{2,1,0:T(8,128)(2,1)}, bf16[16,128,256]{2,1,0:T(8,128)(2,1)}, u32[]{:S(2)}, u32[]{:S(2)}) collective-permute-start(bf16[16,128,256]{2,1,0:T(8,128)(2,1)} %copy-done.14), channel_id=1, source_target_pairs={{0,4},{4,0},{8,12},{12,8},{1,5},{5,1},{9,13},{13,9},{2,6},{6,2},{1... | collective-permute-start | bytes 3145736 | tf_op jit(solution)/shard_map/ppermute | solution.py:24
  226.4 104.5 %collective-permute-start.22 = (bf16[16,128,256]{2,1,0:T(8,128)(2,1)}, bf16[16,128,256]{2,1,0:T(8,128)(2,1)}, u32[]{:S(2)}, u32[]{:S(2)}) collective-permute-start(bf16[16,128,256]{2,1,0:T(8,128)(2,1)} %copy-done.11), channel_id=1, source_target_pairs={{0,8},{4,12},{8,0},{12,4},{1,9},{5,13},{9,1},{13,5},{2,10},{6,14},... | collective-permute-start | bytes 3145736 | tf_op jit(solution)/shard_map/ppermute | solution.py:24
  296.7 34.4 %collective-permute-start.21 = (bf16[16,128,256]{2,1,0:T(8,128)(2,1)}, bf16[16,128,256]{2,1,0:T(8,128)(2,1)}, u32[]{:S(2)}, u32[]{:S(2)}) collective-permute-start(bf16[16,128,256]{2,1,0:T(8,128)(2,1)} %copy-done.10), channel_id=1, source_target_pairs={{0,12},{4,8},{8,4},{12,0},{1,13},{5,9},{9,5},{13,1},{2,14},{6,10},... | collective-permute-start | bytes 3145736 | tf_op jit(solution)/shard_map/ppermute | solution.py:24
  298.9 33.6 %collective-permute-start.20 = (bf16[16,128,256]{2,1,0:T(8,128)(2,1)}, bf16[16,128,256]{2,1,0:T(8,128)(2,1)}, u32[]{:S(2)}, u32[]{:S(2)}) collective-permute-start(bf16[16,128,256]{2,1,0:T(8,128)(2,1)} %copy-done.12), channel_id=1, source_target_pairs={{0,4},{4,0},{8,12},{12,8},{1,5},{5,1},{9,13},{13,9},{2,6},{6,2},{1... | collective-permute-start | bytes 3145736 | tf_op jit(solution)/shard_map/ppermute | solution.py:24
  299.2 1.9 copy-start.21
  329.0 65.7 %collective-permute-start.19 = (bf16[16,128,256]{2,1,0:T(8,128)(2,1)}, bf16[16,128,256]{2,1,0:T(8,128)(2,1)}, u32[]{:S(2)}, u32[]{:S(2)}) collective-permute-start(bf16[16,128,256]{2,1,0:T(8,128)(2,1)} %copy-done.8), channel_id=1, source_target_pairs={{0,8},{4,12},{8,0},{12,4},{1,9},{5,13},{9,1},{13,5},{2,10},{6,14},... | collective-permute-start | bytes 3145736 | tf_op jit(solution)/shard_map/ppermute | solution.py:24
  330.2 70.6 %collective-permute-start.18 = (bf16[16,128,256]{2,1,0:T(8,128)(2,1)}, bf16[16,128,256]{2,1,0:T(8,128)(2,1)}, u32[]{:S(2)}, u32[]{:S(2)}) collective-permute-start(bf16[16,128,256]{2,1,0:T(8,128)(2,1)} %copy-done.6), channel_id=1, source_target_pairs={{0,12},{4,8},{8,4},{12,0},{1,13},{5,9},{9,5},{13,1},{2,14},{6,10},... | collective-permute-start | bytes 3145736 | tf_op jit(solution)/shard_map/ppermute | solution.py:24
  330.8 80.2 %collective-permute-start.17 = (bf16[16,128,256]{2,1,0:T(8,128)(2,1)}, bf16[16,128,256]{2,1,0:T(8,128)(2,1)}, u32[]{:S(2)}, u32[]{:S(2)}) collective-permute-start(bf16[16,128,256]{2,1,0:T(8,128)(2,1)} %copy-done.9), channel_id=1, source_target_pairs={{0,4},{4,0},{8,12},{12,8},{1,5},{5,1},{9,13},{13,9},{2,6},{6,2},{1... | collective-permute-start | bytes 3145736 | tf_op jit(solution)/shard_map/ppermute | solution.py:24
  331.1 86.2 %collective-permute-start.16 = (bf16[16,128,256]{2,1,0:T(8,128)(2,1)}, bf16[16,128,256]{2,1,0:T(8,128)(2,1)}, u32[]{:S(2)}, u32[]{:S(2)}) collective-permute-start(bf16[16,128,256]{2,1,0:T(8,128)(2,1)} %copy-done.7), channel_id=1, source_target_pairs={{0,8},{4,12},{8,0},{12,4},{1,9},{5,13},{9,1},{13,5},{2,10},{6,14},... | collective-permute-start | bytes 3145736 | tf_op jit(solution)/shard_map/ppermute | solution.py:24
  332.5 91.0 %collective-permute-start.15 = (bf16[16,128,256]{2,1,0:T(8,128)(2,1)}, bf16[16,128,256]{2,1,0:T(8,128)(2,1)}, u32[]{:S(2)}, u32[]{:S(2)}) collective-permute-start(bf16[16,128,256]{2,1,0:T(8,128)(2,1)} %copy-done.5), channel_id=1, source_target_pairs={{0,12},{4,8},{8,4},{12,0},{1,13},{5,9},{9,5},{13,1},{2,14},{6,10},... | collective-permute-start | bytes 3145736 | tf_op jit(solution)/shard_map/ppermute | solution.py:24
  337.9 1.2 copy-start.1
  (8 other events, 7.4 us)
Sparse Core Ops, SparseCore 0:
  223.3 33.4 all-reduce.2
